TPU v7x, 256 devices: a whole 4x4x8 slice. The times are simulated.
256 devices in a mesh: dp: 256 (over x, z, y, core).
Axes of the slice: x: 4, y: 4, z: 8, core: 2. Of those that a mesh axis runs over, the one named last changes fastest.
Arguments:
- image_features: bfloat16 [32768, 1152], P('dp'), may hold values from -0.59765625 to 0.59765625
- text_features: bfloat16 [32768, 1152], P('dp'), may hold values from -0.59765625 to 0.59765625
- projections: bfloat16 [2304, 1152], P('dp'), may hold values from -0.1875 to 0.1875
- labels: int32 [32768], P('dp'), may hold values from 0 to 32767, as said below
Outputs:
- image_grad: float32 [32768, 1152], P('dp')
- text_grad: float32 [32768, 1152], P('dp')
Inputs may be any that keep to these rules, and one draw needn't show every extreme that they name: For each block k of 128 rows, the labels are the 128 text rows of one block (k - s) mod 256, each once, with s between 0 and 31 drawn for each block.
All inputs are finite; a program needn't handle non-finite values.
Results may differ from a plain program's by a relative error of at most 0.01.
Values may be sent and summed in bfloat16 or wider, within the bound.
No kernel may reach another device: no remote copies, remote signals or barrier semaphores. Data moves between devices by JAX's collectives and lax.ppermute only.
A program may use at most 128 MiB of HBM per device.

v0:
```python
import jax
import jax.numpy as jnp
from jax import lax
from jax.sharding import PartitionSpec as P

REACH = 32


logit_scale = 10.0
logit_bias = -2.0
eps = 1e-06
contract_last = (((1,), (1,)), ((), ()))
contract_first = (((0,), (0,)), ((), ()))


def from_behind(value, axis, steps):
    count = lax.axis_size(axis)
    pairs = [(source, (source + steps) % count) for source in range(count)]
    return lax.ppermute(value, axis, pairs)


def normalize(raw):
    norm = jnp.sqrt(jnp.sum(raw * raw, axis=-1, keepdims=True) + eps)
    return (raw / norm, norm)


def unproject(unit, norm, grad):
    inner = jnp.sum(unit * grad, axis=-1, keepdims=True)
    return ((grad - unit * inner) / norm).astype(jnp.bfloat16)


def coefficients(left, right, left_labels, right_ids):
    logits = (
        logit_scale
        * lax.dot_general(left, right, contract_last, preferred_element_type=jnp.float32)
        + logit_bias
    )
    positive = (left_labels[:, None] == right_ids[None, :]).astype(jnp.float32)
    return (jax.nn.sigmoid(logits) - positive).astype(jnp.bfloat16)


def next_text(block):
    return from_behind(block, "dp", 1)


def next_partial(partial_value):
    return from_behind(partial_value, "dp", 1)


def send_home(partial_value, distance):
    return from_behind(partial_value.astype(jnp.bfloat16), "dp", -distance).astype(
        partial_value.dtype
    )


def per_device(image_features, text_features, projections, labels):
    rows, width_in = image_features.shape
    count = lax.axis_size("dp")
    index = lax.axis_index("dp")
    shifts = min(REACH, count // 2)
    whole = lax.all_gather(projections, "dp", axis=0, tiled=True)
    image_weight = whole[:width_in]
    text_weight = whole[width_in:]
    image_unit, image_norm = normalize(
        jnp.dot(image_features, image_weight, preferred_element_type=jnp.float32)
    )
    text_unit, text_norm = normalize(
        jnp.dot(text_features, text_weight, preferred_element_type=jnp.float32)
    )
    image_emb = image_unit.astype(jnp.bfloat16)
    text_emb = text_unit.astype(jnp.bfloat16)
    width = image_emb.shape[1]
    positions = jnp.arange(rows, dtype=jnp.int32)
    zeros = jnp.zeros((rows, width), jnp.float32)

    def pair_terms(block, offset):
        text_ids = (index - offset) % count * rows + positions
        coeff = coefficients(image_emb, block, labels, text_ids)
        image_part = logit_scale * jnp.dot(coeff, block, preferred_element_type=jnp.float32)
        text_part = logit_scale * lax.dot_general(
            coeff, image_emb, contract_first, preferred_element_type=jnp.float32
        )
        return (image_part, text_part)

    def forward_step(offset, state):
        block, partial_value, total = state
        image_part, text_part = pair_terms(block, offset)
        return (next_text(block), next_partial(partial_value + text_part), total + image_part)

    block, partial_value, image_acc = lax.fori_loop(
        0, shifts - 1, forward_step, (text_emb, zeros, zeros)
    )
    image_part, text_part = pair_terms(block, shifts - 1)
    image_acc = image_acc + image_part
    partial_value = partial_value + text_part
    text_acc = send_home(partial_value, shifts - 1)
    image_draw = unproject(image_unit, image_norm, image_acc)
    text_draw = unproject(text_unit, text_norm, text_acc)
    image_grad = lax.dot_general(
        image_draw, image_weight, contract_last, preferred_element_type=jnp.float32
    )
    text_grad = lax.dot_general(
        text_draw, text_weight, contract_last, preferred_element_type=jnp.float32
    )
    return (image_grad, text_grad)


def solution(mesh):
    placed = (P("dp", None), P("dp", None), P("dp", None), P("dp"))
    return jax.shard_map(
        per_device,
        mesh=mesh,
        in_specs=placed,
        out_specs=(P("dp", None), P("dp", None)),
        check_vma=False,
    )
```

profile of v0, /device:TPU:0, one launch (start us, length us, event | category | flops | bytes accessed | tf_op | source)
XLA Modules:
  0.0 756.3 jit_solution(15745396621491654764)
XLA Ops:
  8.0 123.4 %all-gather.3.cloned.1.call-done = bf16[256,9,1152]{2,1,0:T(8,128)(2,1)} async-done(((bf16[1,9,1152]{2,1,0:T(8,128)(2,1)}), bf16[256,9,1152]{2,1,0:T(8,128)(2,1)}) %all-gather.3.cloned.1.call-update) | async-done | bytes 5308432 | tf_op jit(solution)/shard_map/all_gather | solution.py:61
  152.9 582.0 %while.20 = (s32[]{:T(128)}, bf16[128,1152]{1,0:T(8,128)(2,1)S(1)}, f32[128,1152]{1,0:T(8,128)S(1)}, f32[128,1152]{1,0:T(8,128)S(1)}, bf16[128,1152]{1,0:T(8,128...) while((s32[]{:T(128)}, bf16[128,1152]{1,0:T(8,128)(2,1)S(1)}, ...), condition=%wide.region_3.4_spmd.clone, body=%wide.region_2.3_spmd.clone.sunk | while | flops 114131088 | bytes 7767896 | solution.py:90
  172.5 17.5 %collective-permute-done = bf16[128,1152]{1,0:T(8,128)(2,1)S(1)} collective-permute-done((bf16[128,1152]{1,0:T(8,128)(2,1)S(1)}, bf16[128,1152]{1,0:T(8,128)(2,1)S(1)}, u32[]{:S(2)}, u32[]{:S(2)}) %collective-permute-start) | collective-permute-done | bytes 294944 | tf_op jit(solution)/shard_map/while/body/eval_jaxpr/ppermute | solution.py:19
  191.1 17.5 %collective-permute-done = bf16[128,1152]{1,0:T(8,128)(2,1)S(1)} collective-permute-done((bf16[128,1152]{1,0:T(8,128)(2,1)S(1)}, bf16[128,1152]{1,0:T(8,128)(2,1)S(1)}, u32[]{:S(2)}, u32[]{:S(2)}) %collective-permute-start) | collective-permute-done | bytes 294944 | tf_op jit(solution)/shard_map/while/body/eval_jaxpr/ppermute | solution.py:19
  209.6 17.5 %collective-permute-done = bf16[128,1152]{1,0:T(8,128)(2,1)S(1)} collective-permute-done((bf16[128,1152]{1,0:T(8,128)(2,1)S(1)}, bf16[128,1152]{1,0:T(8,128)(2,1)S(1)}, u32[]{:S(2)}, u32[]{:S(2)}) %collective-permute-start) | collective-permute-done | bytes 294944 | tf_op jit(solution)/shard_map/while/body/eval_jaxpr/ppermute | solution.py:19
  228.2 17.5 %collective-permute-done = bf16[128,1152]{1,0:T(8,128)(2,1)S(1)} collective-permute-done((bf16[128,1152]{1,0:T(8,128)(2,1)S(1)}, bf16[128,1152]{1,0:T(8,128)(2,1)S(1)}, u32[]{:S(2)}, u32[]{:S(2)}) %collective-permute-start) | collective-permute-done | bytes 294944 | tf_op jit(solution)/shard_map/while/body/eval_jaxpr/ppermute | solution.py:19
  246.8 17.5 %collective-permute-done = bf16[128,1152]{1,0:T(8,128)(2,1)S(1)} collective-permute-done((bf16[128,1152]{1,0:T(8,128)(2,1)S(1)}, bf16[128,1152]{1,0:T(8,128)(2,1)S(1)}, u32[]{:S(2)}, u32[]{:S(2)}) %collective-permute-start) | collective-permute-done | bytes 294944 | tf_op jit(solution)/shard_map/while/body/eval_jaxpr/ppermute | solution.py:19
  265.4 17.5 %collective-permute-done = bf16[128,1152]{1,0:T(8,128)(2,1)S(1)} collective-permute-done((bf16[128,1152]{1,0:T(8,128)(2,1)S(1)}, bf16[128,1152]{1,0:T(8,128)(2,1)S(1)}, u32[]{:S(2)}, u32[]{:S(2)}) %collective-permute-start) | collective-permute-done | bytes 294944 | tf_op jit(solution)/shard_map/while/body/eval_jaxpr/ppermute | solution.py:19
  283.9 17.5 %collective-permute-done = bf16[128,1152]{1,0:T(8,128)(2,1)S(1)} collective-permute-done((bf16[128,1152]{1,0:T(8,128)(2,1)S(1)}, bf16[128,1152]{1,0:T(8,128)(2,1)S(1)}, u32[]{:S(2)}, u32[]{:S(2)}) %collective-permute-start) | collective-permute-done | bytes 294944 | tf_op jit(solution)/shard_map/while/body/eval_jaxpr/ppermute | solution.py:19
  302.5 17.5 %collective-permute-done = bf16[128,1152]{1,0:T(8,128)(2,1)S(1)} collective-permute-done((bf16[128,1152]{1,0:T(8,128)(2,1)S(1)}, bf16[128,1152]{1,0:T(8,128)(2,1)S(1)}, u32[]{:S(2)}, u32[]{:S(2)}) %collective-permute-start) | collective-permute-done | bytes 294944 | tf_op jit(solution)/shard_map/while/body/eval_jaxpr/ppermute | solution.py:19
  321.1 17.5 %collective-permute-done = bf16[128,1152]{1,0:T(8,128)(2,1)S(1)} collective-permute-done((bf16[128,1152]{1,0:T(8,128)(2,1)S(1)}, bf16[128,1152]{1,0:T(8,128)(2,1)S(1)}, u32[]{:S(2)}, u32[]{:S(2)}) %collective-permute-start) | collective-permute-done | bytes 294944 | tf_op jit(solution)/shard_map/while/body/eval_jaxpr/ppermute | solution.py:19
  339.6 17.5 %collective-permute-done = bf16[128,1152]{1,0:T(8,128)(2,1)S(1)} collective-permute-done((bf16[128,1152]{1,0:T(8,128)(2,1)S(1)}, bf16[128,1152]{1,0:T(8,128)(2,1)S(1)}, u32[]{:S(2)}, u32[]{:S(2)}) %collective-permute-start) | collective-permute-done | bytes 294944 | tf_op jit(solution)/shard_map/while/body/eval_jaxpr/ppermute | solution.py:19
  358.2 17.5 %collective-permute-done = bf16[128,1152]{1,0:T(8,128)(2,1)S(1)} collective-permute-done((bf16[128,1152]{1,0:T(8,128)(2,1)S(1)}, bf16[128,1152]{1,0:T(8,128)(2,1)S(1)}, u32[]{:S(2)}, u32[]{:S(2)}) %collective-permute-start) | collective-permute-done | bytes 294944 | tf_op jit(solution)/shard_map/while/body/eval_jaxpr/ppermute | solution.py:19
  376.8 17.5 %collective-permute-done = bf16[128,1152]{1,0:T(8,128)(2,1)S(1)} collective-permute-done((bf16[128,1152]{1,0:T(8,128)(2,1)S(1)}, bf16[128,1152]{1,0:T(8,128)(2,1)S(1)}, u32[]{:S(2)}, u32[]{:S(2)}) %collective-permute-start) | collective-permute-done | bytes 294944 | tf_op jit(solution)/shard_map/while/body/eval_jaxpr/ppermute | solution.py:19
  395.3 17.5 %collective-permute-done = bf16[128,1152]{1,0:T(8,128)(2,1)S(1)} collective-permute-done((bf16[128,1152]{1,0:T(8,128)(2,1)S(1)}, bf16[128,1152]{1,0:T(8,128)(2,1)S(1)}, u32[]{:S(2)}, u32[]{:S(2)}) %collective-permute-start) | collective-permute-done | bytes 294944 | tf_op jit(solution)/shard_map/while/body/eval_jaxpr/ppermute | solution.py:19
  413.9 17.5 %collective-permute-done = bf16[128,1152]{1,0:T(8,128)(2,1)S(1)} collective-permute-done((bf16[128,1152]{1,0:T(8,128)(2,1)S(1)}, bf16[128,1152]{1,0:T(8,128)(2,1)S(1)}, u32[]{:S(2)}, u32[]{:S(2)}) %collective-permute-start) | collective-permute-done | bytes 294944 | tf_op jit(solution)/shard_map/while/body/eval_jaxpr/ppermute | solution.py:19
  432.5 17.5 %collective-permute-done = bf16[128,1152]{1,0:T(8,128)(2,1)S(1)} collective-permute-done((bf16[128,1152]{1,0:T(8,128)(2,1)S(1)}, bf16[128,1152]{1,0:T(8,128)(2,1)S(1)}, u32[]{:S(2)}, u32[]{:S(2)}) %collective-permute-start) | collective-permute-done | bytes 294944 | tf_op jit(solution)/shard_map/while/body/eval_jaxpr/ppermute | solution.py:19
  451.0 17.5 %collective-permute-done = bf16[128,1152]{1,0:T(8,128)(2,1)S(1)} collective-permute-done((bf16[128,1152]{1,0:T(8,128)(2,1)S(1)}, bf16[128,1152]{1,0:T(8,128)(2,1)S(1)}, u32[]{:S(2)}, u32[]{:S(2)}) %collective-permute-start) | collective-permute-done | bytes 294944 | tf_op jit(solution)/shard_map/while/body/eval_jaxpr/ppermute | solution.py:19
  469.6 17.5 %collective-permute-done = bf16[128,1152]{1,0:T(8,128)(2,1)S(1)} collective-permute-done((bf16[128,1152]{1,0:T(8,128)(2,1)S(1)}, bf16[128,1152]{1,0:T(8,128)(2,1)S(1)}, u32[]{:S(2)}, u32[]{:S(2)}) %collective-permute-start) | collective-permute-done | bytes 294944 | tf_op jit(solution)/shard_map/while/body/eval_jaxpr/ppermute | solution.py:19
  488.2 17.5 %collective-permute-done = bf16[128,1152]{1,0:T(8,128)(2,1)S(1)} collective-permute-done((bf16[128,1152]{1,0:T(8,128)(2,1)S(1)}, bf16[128,1152]{1,0:T(8,128)(2,1)S(1)}, u32[]{:S(2)}, u32[]{:S(2)}) %collective-permute-start) | collective-permute-done | bytes 294944 | tf_op jit(solution)/shard_map/while/body/eval_jaxpr/ppermute | solution.py:19
  506.7 17.5 %collective-permute-done = bf16[128,1152]{1,0:T(8,128)(2,1)S(1)} collective-permute-done((bf16[128,1152]{1,0:T(8,128)(2,1)S(1)}, bf16[128,1152]{1,0:T(8,128)(2,1)S(1)}, u32[]{:S(2)}, u32[]{:S(2)}) %collective-permute-start) | collective-permute-done | bytes 294944 | tf_op jit(solution)/shard_map/while/body/eval_jaxpr/ppermute | solution.py:19
  525.3 17.5 %collective-permute-done = bf16[128,1152]{1,0:T(8,128)(2,1)S(1)} collective-permute-done((bf16[128,1152]{1,0:T(8,128)(2,1)S(1)}, bf16[128,1152]{1,0:T(8,128)(2,1)S(1)}, u32[]{:S(2)}, u32[]{:S(2)}) %collective-permute-start) | collective-permute-done | bytes 294944 | tf_op jit(solution)/shard_map/while/body/eval_jaxpr/ppermute | solution.py:19
  543.9 17.5 %collective-permute-done = bf16[128,1152]{1,0:T(8,128)(2,1)S(1)} collective-permute-done((bf16[128,1152]{1,0:T(8,128)(2,1)S(1)}, bf16[128,1152]{1,0:T(8,128)(2,1)S(1)}, u32[]{:S(2)}, u32[]{:S(2)}) %collective-permute-start) | collective-permute-done | bytes 294944 | tf_op jit(solution)/shard_map/while/body/eval_jaxpr/ppermute | solution.py:19
  562.4 17.5 %collective-permute-done = bf16[128,1152]{1,0:T(8,128)(2,1)S(1)} collective-permute-done((bf16[128,1152]{1,0:T(8,128)(2,1)S(1)}, bf16[128,1152]{1,0:T(8,128)(2,1)S(1)}, u32[]{:S(2)}, u32[]{:S(2)}) %collective-permute-start) | collective-permute-done | bytes 294944 | tf_op jit(solution)/shard_map/while/body/eval_jaxpr/ppermute | solution.py:19
  581.0 17.5 %collective-permute-done = bf16[128,1152]{1,0:T(8,128)(2,1)S(1)} collective-permute-done((bf16[128,1152]{1,0:T(8,128)(2,1)S(1)}, bf16[128,1152]{1,0:T(8,128)(2,1)S(1)}, u32[]{:S(2)}, u32[]{:S(2)}) %collective-permute-start) | collective-permute-done | bytes 294944 | tf_op jit(solution)/shard_map/while/body/eval_jaxpr/ppermute | solution.py:19
  599.6 17.5 %collective-permute-done = bf16[128,1152]{1,0:T(8,128)(2,1)S(1)} collective-permute-done((bf16[128,1152]{1,0:T(8,128)(2,1)S(1)}, bf16[128,1152]{1,0:T(8,128)(2,1)S(1)}, u32[]{:S(2)}, u32[]{:S(2)}) %collective-permute-start) | collective-permute-done | bytes 294944 | tf_op jit(solution)/shard_map/while/body/eval_jaxpr/ppermute | solution.py:19
  618.2 20.7 %collective-permute-done = bf16[128,1152]{1,0:T(8,128)(2,1)S(1)} collective-permute-done((bf16[128,1152]{1,0:T(8,128)(2,1)S(1)}, bf16[128,1152]{1,0:T(8,128)(2,1)S(1)}, u32[]{:S(2)}, u32[]{:S(2)}) %collective-permute-start) | collective-permute-done | bytes 294944 | tf_op jit(solution)/shard_map/while/body/eval_jaxpr/ppermute | solution.py:19
  639.9 17.5 %collective-permute-done = bf16[128,1152]{1,0:T(8,128)(2,1)S(1)} collective-permute-done((bf16[128,1152]{1,0:T(8,128)(2,1)S(1)}, bf16[128,1152]{1,0:T(8,128)(2,1)S(1)}, u32[]{:S(2)}, u32[]{:S(2)}) %collective-permute-start) | collective-permute-done | bytes 294944 | tf_op jit(solution)/shard_map/while/body/eval_jaxpr/ppermute | solution.py:19
  658.4 20.7 %collective-permute-done = bf16[128,1152]{1,0:T(8,128)(2,1)S(1)} collective-permute-done((bf16[128,1152]{1,0:T(8,128)(2,1)S(1)}, bf16[128,1152]{1,0:T(8,128)(2,1)S(1)}, u32[]{:S(2)}, u32[]{:S(2)}) %collective-permute-start) | collective-permute-done | bytes 294944 | tf_op jit(solution)/shard_map/while/body/eval_jaxpr/ppermute | solution.py:19
  680.2 17.5 %collective-permute-done = bf16[128,1152]{1,0:T(8,128)(2,1)S(1)} collective-permute-done((bf16[128,1152]{1,0:T(8,128)(2,1)S(1)}, bf16[128,1152]{1,0:T(8,128)(2,1)S(1)}, u32[]{:S(2)}, u32[]{:S(2)}) %collective-permute-start) | collective-permute-done | bytes 294944 | tf_op jit(solution)/shard_map/while/body/eval_jaxpr/ppermute | solution.py:19
  698.7 17.5 %collective-permute-done = bf16[128,1152]{1,0:T(8,128)(2,1)S(1)} collective-permute-done((bf16[128,1152]{1,0:T(8,128)(2,1)S(1)}, bf16[128,1152]{1,0:T(8,128)(2,1)S(1)}, u32[]{:S(2)}, u32[]{:S(2)}) %collective-permute-start) | collective-permute-done | bytes 294944 | tf_op jit(solution)/shard_map/while/body/eval_jaxpr/ppermute | solution.py:19
  717.3 17.5 %collective-permute-done = bf16[128,1152]{1,0:T(8,128)(2,1)S(1)} collective-permute-done((bf16[128,1152]{1,0:T(8,128)(2,1)S(1)}, bf16[128,1152]{1,0:T(8,128)(2,1)S(1)}, u32[]{:S(2)}, u32[]{:S(2)}) %collective-permute-start) | collective-permute-done | bytes 294944 | tf_op jit(solution)/shard_map/while/body/eval_jaxpr/ppermute | solution.py:19
  (290 shorter events, 84.9 us)
Async XLA Ops:
  7.2 124.2 %all-gather.3.cloned.1.call-start = ((), (), s32[]{:S(2)}) async-start(), calls=%async_computation | async-start | bytes 9474048 | tf_op jit(solution)/shard_map/all_gather | solution.py:61
  153.5 18.0 %collective-permute-start.1 = (f32[128,1152]{1,0:T(8,128)S(1)}, f32[128,1152]{1,0:T(8,128)S(1)}, u32[]{:S(2)}, u32[]{:S(2)}) collective-permute-start(f32[128,1152]{1,0:T(8,128)S(1)} %fusion.68), channel_id=1, source_target_pairs={{0,1},{1,2},{2,3},{3,4},{4,5},{5,6},{6,7},{7,8},{8,9},{9,10},{10,1... | collective-permute-start | bytes 1769480 | tf_op jit(solution)/shard_map/while/body/eval_jaxpr/ppermute | solution.py:19
  172.0 18.0 %collective-permute-start.1 = (f32[128,1152]{1,0:T(8,128)S(1)}, f32[128,1152]{1,0:T(8,128)S(1)}, u32[]{:S(2)}, u32[]{:S(2)}) collective-permute-start(f32[128,1152]{1,0:T(8,128)S(1)} %fusion.68), channel_id=1, source_target_pairs={{0,1},{1,2},{2,3},{3,4},{4,5},{5,6},{6,7},{7,8},{8,9},{9,10},{10,1... | collective-permute-start | bytes 1769480 | tf_op jit(solution)/shard_map/while/body/eval_jaxpr/ppermute | solution.py:19
  190.6 18.0 %collective-permute-start.1 = (f32[128,1152]{1,0:T(8,128)S(1)}, f32[128,1152]{1,0:T(8,128)S(1)}, u32[]{:S(2)}, u32[]{:S(2)}) collective-permute-start(f32[128,1152]{1,0:T(8,128)S(1)} %fusion.68), channel_id=1, source_target_pairs={{0,1},{1,2},{2,3},{3,4},{4,5},{5,6},{6,7},{7,8},{8,9},{9,10},{10,1... | collective-permute-start | bytes 1769480 | tf_op jit(solution)/shard_map/while/body/eval_jaxpr/ppermute | solution.py:19
  209.2 18.0 %collective-permute-start.1 = (f32[128,1152]{1,0:T(8,128)S(1)}, f32[128,1152]{1,0:T(8,128)S(1)}, u32[]{:S(2)}, u32[]{:S(2)}) collective-permute-start(f32[128,1152]{1,0:T(8,128)S(1)} %fusion.68), channel_id=1, source_target_pairs={{0,1},{1,2},{2,3},{3,4},{4,5},{5,6},{6,7},{7,8},{8,9},{9,10},{10,1... | collective-permute-start | bytes 1769480 | tf_op jit(solution)/shard_map/while/body/eval_jaxpr/ppermute | solution.py:19
  227.7 18.0 %collective-permute-start.1 = (f32[128,1152]{1,0:T(8,128)S(1)}, f32[128,1152]{1,0:T(8,128)S(1)}, u32[]{:S(2)}, u32[]{:S(2)}) collective-permute-start(f32[128,1152]{1,0:T(8,128)S(1)} %fusion.68), channel_id=1, source_target_pairs={{0,1},{1,2},{2,3},{3,4},{4,5},{5,6},{6,7},{7,8},{8,9},{9,10},{10,1... | collective-permute-start | bytes 1769480 | tf_op jit(solution)/shard_map/while/body/eval_jaxpr/ppermute | solution.py:19
  246.3 18.0 %collective-permute-start.1 = (f32[128,1152]{1,0:T(8,128)S(1)}, f32[128,1152]{1,0:T(8,128)S(1)}, u32[]{:S(2)}, u32[]{:S(2)}) collective-permute-start(f32[128,1152]{1,0:T(8,128)S(1)} %fusion.68), channel_id=1, source_target_pairs={{0,1},{1,2},{2,3},{3,4},{4,5},{5,6},{6,7},{7,8},{8,9},{9,10},{10,1... | collective-permute-start | bytes 1769480 | tf_op jit(solution)/shard_map/while/body/eval_jaxpr/ppermute | solution.py:19
  264.9 18.0 %collective-permute-start.1 = (f32[128,1152]{1,0:T(8,128)S(1)}, f32[128,1152]{1,0:T(8,128)S(1)}, u32[]{:S(2)}, u32[]{:S(2)}) collective-permute-start(f32[128,1152]{1,0:T(8,128)S(1)} %fusion.68), channel_id=1, source_target_pairs={{0,1},{1,2},{2,3},{3,4},{4,5},{5,6},{6,7},{7,8},{8,9},{9,10},{10,1... | collective-permute-start | bytes 1769480 | tf_op jit(solution)/shard_map/while/body/eval_jaxpr/ppermute | solution.py:19
  283.5 18.0 %collective-permute-start.1 = (f32[128,1152]{1,0:T(8,128)S(1)}, f32[128,1152]{1,0:T(8,128)S(1)}, u32[]{:S(2)}, u32[]{:S(2)}) collective-permute-start(f32[128,1152]{1,0:T(8,128)S(1)} %fusion.68), channel_id=1, source_target_pairs={{0,1},{1,2},{2,3},{3,4},{4,5},{5,6},{6,7},{7,8},{8,9},{9,10},{10,1... | collective-permute-start | bytes 1769480 | tf_op jit(solution)/shard_map/while/body/eval_jaxpr/ppermute | solution.py:19
  302.0 18.0 %collective-permute-start.1 = (f32[128,1152]{1,0:T(8,128)S(1)}, f32[128,1152]{1,0:T(8,128)S(1)}, u32[]{:S(2)}, u32[]{:S(2)}) collective-permute-start(f32[128,1152]{1,0:T(8,128)S(1)} %fusion.68), channel_id=1, source_target_pairs={{0,1},{1,2},{2,3},{3,4},{4,5},{5,6},{6,7},{7,8},{8,9},{9,10},{10,1... | collective-permute-start | bytes 1769480 | tf_op jit(solution)/shard_map/while/body/eval_jaxpr/ppermute | solution.py:19
  320.6 18.0 %collective-permute-start.1 = (f32[128,1152]{1,0:T(8,128)S(1)}, f32[128,1152]{1,0:T(8,128)S(1)}, u32[]{:S(2)}, u32[]{:S(2)}) collective-permute-start(f32[128,1152]{1,0:T(8,128)S(1)} %fusion.68), channel_id=1, source_target_pairs={{0,1},{1,2},{2,3},{3,4},{4,5},{5,6},{6,7},{7,8},{8,9},{9,10},{10,1... | collective-permute-start | bytes 1769480 | tf_op jit(solution)/shard_map/while/body/eval_jaxpr/ppermute | solution.py:19
  339.2 18.0 %collective-permute-start.1 = (f32[128,1152]{1,0:T(8,128)S(1)}, f32[128,1152]{1,0:T(8,128)S(1)}, u32[]{:S(2)}, u32[]{:S(2)}) collective-permute-start(f32[128,1152]{1,0:T(8,128)S(1)} %fusion.68), channel_id=1, source_target_pairs={{0,1},{1,2},{2,3},{3,4},{4,5},{5,6},{6,7},{7,8},{8,9},{9,10},{10,1... | collective-permute-start | bytes 1769480 | tf_op jit(solution)/shard_map/while/body/eval_jaxpr/ppermute | solution.py:19
  357.7 18.0 %collective-permute-start.1 = (f32[128,1152]{1,0:T(8,128)S(1)}, f32[128,1152]{1,0:T(8,128)S(1)}, u32[]{:S(2)}, u32[]{:S(2)}) collective-permute-start(f32[128,1152]{1,0:T(8,128)S(1)} %fusion.68), channel_id=1, source_target_pairs={{0,1},{1,2},{2,3},{3,4},{4,5},{5,6},{6,7},{7,8},{8,9},{9,10},{10,1... | collective-permute-start | bytes 1769480 | tf_op jit(solution)/shard_map/while/body/eval_jaxpr/ppermute | solution.py:19
  376.3 18.0 %collective-permute-start.1 = (f32[128,1152]{1,0:T(8,128)S(1)}, f32[128,1152]{1,0:T(8,128)S(1)}, u32[]{:S(2)}, u32[]{:S(2)}) collective-permute-start(f32[128,1152]{1,0:T(8,128)S(1)} %fusion.68), channel_id=1, source_target_pairs={{0,1},{1,2},{2,3},{3,4},{4,5},{5,6},{6,7},{7,8},{8,9},{9,10},{10,1... | collective-permute-start | bytes 1769480 | tf_op jit(solution)/shard_map/while/body/eval_jaxpr/ppermute | solution.py:19
  394.9 18.0 %collective-permute-start.1 = (f32[128,1152]{1,0:T(8,128)S(1)}, f32[128,1152]{1,0:T(8,128)S(1)}, u32[]{:S(2)}, u32[]{:S(2)}) collective-permute-start(f32[128,1152]{1,0:T(8,128)S(1)} %fusion.68), channel_id=1, source_target_pairs={{0,1},{1,2},{2,3},{3,4},{4,5},{5,6},{6,7},{7,8},{8,9},{9,10},{10,1... | collective-permute-start | bytes 1769480 | tf_op jit(solution)/shard_map/while/body/eval_jaxpr/ppermute | solution.py:19
  413.4 18.0 %collective-permute-start.1 = (f32[128,1152]{1,0:T(8,128)S(1)}, f32[128,1152]{1,0:T(8,128)S(1)}, u32[]{:S(2)}, u32[]{:S(2)}) collective-permute-start(f32[128,1152]{1,0:T(8,128)S(1)} %fusion.68), channel_id=1, source_target_pairs={{0,1},{1,2},{2,3},{3,4},{4,5},{5,6},{6,7},{7,8},{8,9},{9,10},{10,1... | collective-permute-start | bytes 1769480 | tf_op jit(solution)/shard_map/while/body/eval_jaxpr/ppermute | solution.py:19
  432.0 18.0 %collective-permute-start.1 = (f32[128,1152]{1,0:T(8,128)S(1)}, f32[128,1152]{1,0:T(8,128)S(1)}, u32[]{:S(2)}, u32[]{:S(2)}) collective-permute-start(f32[128,1152]{1,0:T(8,128)S(1)} %fusion.68), channel_id=1, source_target_pairs={{0,1},{1,2},{2,3},{3,4},{4,5},{5,6},{6,7},{7,8},{8,9},{9,10},{10,1... | collective-permute-start | bytes 1769480 | tf_op jit(solution)/shard_map/while/body/eval_jaxpr/ppermute | solution.py:19
  450.6 18.0 %collective-permute-start.1 = (f32[128,1152]{1,0:T(8,128)S(1)}, f32[128,1152]{1,0:T(8,128)S(1)}, u32[]{:S(2)}, u32[]{:S(2)}) collective-permute-start(f32[128,1152]{1,0:T(8,128)S(1)} %fusion.68), channel_id=1, source_target_pairs={{0,1},{1,2},{2,3},{3,4},{4,5},{5,6},{6,7},{7,8},{8,9},{9,10},{10,1... | collective-permute-start | bytes 1769480 | tf_op jit(solution)/shard_map/while/body/eval_jaxpr/ppermute | solution.py:19
  469.1 18.0 %collective-permute-start.1 = (f32[128,1152]{1,0:T(8,128)S(1)}, f32[128,1152]{1,0:T(8,128)S(1)}, u32[]{:S(2)}, u32[]{:S(2)}) collective-permute-start(f32[128,1152]{1,0:T(8,128)S(1)} %fusion.68), channel_id=1, source_target_pairs={{0,1},{1,2},{2,3},{3,4},{4,5},{5,6},{6,7},{7,8},{8,9},{9,10},{10,1... | collective-permute-start | bytes 1769480 | tf_op jit(solution)/shard_map/while/body/eval_jaxpr/ppermute | solution.py:19
  487.7 18.0 %collective-permute-start.1 = (f32[128,1152]{1,0:T(8,128)S(1)}, f32[128,1152]{1,0:T(8,128)S(1)}, u32[]{:S(2)}, u32[]{:S(2)}) collective-permute-start(f32[128,1152]{1,0:T(8,128)S(1)} %fusion.68), channel_id=1, source_target_pairs={{0,1},{1,2},{2,3},{3,4},{4,5},{5,6},{6,7},{7,8},{8,9},{9,10},{10,1... | collective-permute-start | bytes 1769480 | tf_op jit(solution)/shard_map/while/body/eval_jaxpr/ppermute | solution.py:19
  506.3 18.0 %collective-permute-start.1 = (f32[128,1152]{1,0:T(8,128)S(1)}, f32[128,1152]{1,0:T(8,128)S(1)}, u32[]{:S(2)}, u32[]{:S(2)}) collective-permute-start(f32[128,1152]{1,0:T(8,128)S(1)} %fusion.68), channel_id=1, source_target_pairs={{0,1},{1,2},{2,3},{3,4},{4,5},{5,6},{6,7},{7,8},{8,9},{9,10},{10,1... | collective-permute-start | bytes 1769480 | tf_op jit(solution)/shard_map/while/body/eval_jaxpr/ppermute | solution.py:19
  524.8 18.0 %collective-permute-start.1 = (f32[128,1152]{1,0:T(8,128)S(1)}, f32[128,1152]{1,0:T(8,128)S(1)}, u32[]{:S(2)}, u32[]{:S(2)}) collective-permute-start(f32[128,1152]{1,0:T(8,128)S(1)} %fusion.68), channel_id=1, source_target_pairs={{0,1},{1,2},{2,3},{3,4},{4,5},{5,6},{6,7},{7,8},{8,9},{9,10},{10,1... | collective-permute-start | bytes 1769480 | tf_op jit(solution)/shard_map/while/body/eval_jaxpr/ppermute | solution.py:19
  543.4 18.0 %collective-permute-start.1 = (f32[128,1152]{1,0:T(8,128)S(1)}, f32[128,1152]{1,0:T(8,128)S(1)}, u32[]{:S(2)}, u32[]{:S(2)}) collective-permute-start(f32[128,1152]{1,0:T(8,128)S(1)} %fusion.68), channel_id=1, source_target_pairs={{0,1},{1,2},{2,3},{3,4},{4,5},{5,6},{6,7},{7,8},{8,9},{9,10},{10,1... | collective-permute-start | bytes 1769480 | tf_op jit(solution)/shard_map/while/body/eval_jaxpr/ppermute | solution.py:19
  562.0 18.0 %collective-permute-start.1 = (f32[128,1152]{1,0:T(8,128)S(1)}, f32[128,1152]{1,0:T(8,128)S(1)}, u32[]{:S(2)}, u32[]{:S(2)}) collective-permute-start(f32[128,1152]{1,0:T(8,128)S(1)} %fusion.68), channel_id=1, source_target_pairs={{0,1},{1,2},{2,3},{3,4},{4,5},{5,6},{6,7},{7,8},{8,9},{9,10},{10,1... | collective-permute-start | bytes 1769480 | tf_op jit(solution)/shard_map/while/body/eval_jaxpr/ppermute | solution.py:19
  580.5 18.0 %collective-permute-start.1 = (f32[128,1152]{1,0:T(8,128)S(1)}, f32[128,1152]{1,0:T(8,128)S(1)}, u32[]{:S(2)}, u32[]{:S(2)}) collective-permute-start(f32[128,1152]{1,0:T(8,128)S(1)} %fusion.68), channel_id=1, source_target_pairs={{0,1},{1,2},{2,3},{3,4},{4,5},{5,6},{6,7},{7,8},{8,9},{9,10},{10,1... | collective-permute-start | bytes 1769480 | tf_op jit(solution)/shard_map/while/body/eval_jaxpr/ppermute | solution.py:19
  599.1 18.0 %collective-permute-start.1 = (f32[128,1152]{1,0:T(8,128)S(1)}, f32[128,1152]{1,0:T(8,128)S(1)}, u32[]{:S(2)}, u32[]{:S(2)}) collective-permute-start(f32[128,1152]{1,0:T(8,128)S(1)} %fusion.68), channel_id=1, source_target_pairs={{0,1},{1,2},{2,3},{3,4},{4,5},{5,6},{6,7},{7,8},{8,9},{9,10},{10,1... | collective-permute-start | bytes 1769480 | tf_op jit(solution)/shard_map/while/body/eval_jaxpr/ppermute | solution.py:19
  617.7 21.1 %collective-permute-start.1 = (f32[128,1152]{1,0:T(8,128)S(1)}, f32[128,1152]{1,0:T(8,128)S(1)}, u32[]{:S(2)}, u32[]{:S(2)}) collective-permute-start(f32[128,1152]{1,0:T(8,128)S(1)} %fusion.68), channel_id=1, source_target_pairs={{0,1},{1,2},{2,3},{3,4},{4,5},{5,6},{6,7},{7,8},{8,9},{9,10},{10,1... | collective-permute-start | bytes 1769480 | tf_op jit(solution)/shard_map/while/body/eval_jaxpr/ppermute | solution.py:19
  617.8 21.0 %collective-permute-start = (bf16[128,1152]{1,0:T(8,128)(2,1)S(1)}, bf16[128,1152]{1,0:T(8,128)(2,1)S(1)}, u32[]{:S(2)}, u32[]{:S(2)}) collective-permute-start(bf16[128,1152]{1,0:T(8,128)(2,1)S(1)} %copy.11), channel_id=1, source_target_pairs={{0,1},{1,2},{2,3},{3,4},{4,5},{5,6},{6,7},{7,8},{8,9},{9,10},{10,1... | collective-permute-start | bytes 884744 | tf_op jit(solution)/shard_map/while/body/eval_jaxpr/ppermute | solution.py:19
  639.4 18.0 %collective-permute-start.1 = (f32[128,1152]{1,0:T(8,128)S(1)}, f32[128,1152]{1,0:T(8,128)S(1)}, u32[]{:S(2)}, u32[]{:S(2)}) collective-permute-start(f32[128,1152]{1,0:T(8,128)S(1)} %fusion.68), channel_id=1, source_target_pairs={{0,1},{1,2},{2,3},{3,4},{4,5},{5,6},{6,7},{7,8},{8,9},{9,10},{10,1... | collective-permute-start | bytes 1769480 | tf_op jit(solution)/shard_map/while/body/eval_jaxpr/ppermute | solution.py:19
  658.0 21.1 %collective-permute-start.1 = (f32[128,1152]{1,0:T(8,128)S(1)}, f32[128,1152]{1,0:T(8,128)S(1)}, u32[]{:S(2)}, u32[]{:S(2)}) collective-permute-start(f32[128,1152]{1,0:T(8,128)S(1)} %fusion.68), channel_id=1, source_target_pairs={{0,1},{1,2},{2,3},{3,4},{4,5},{5,6},{6,7},{7,8},{8,9},{9,10},{10,1... | collective-permute-start | bytes 1769480 | tf_op jit(solution)/shard_map/while/body/eval_jaxpr/ppermute | solution.py:19
  658.1 21.0 %collective-permute-start = (bf16[128,1152]{1,0:T(8,128)(2,1)S(1)}, bf16[128,1152]{1,0:T(8,128)(2,1)S(1)}, u32[]{:S(2)}, u32[]{:S(2)}) collective-permute-start(bf16[128,1152]{1,0:T(8,128)(2,1)S(1)} %copy.11), channel_id=1, source_target_pairs={{0,1},{1,2},{2,3},{3,4},{4,5},{5,6},{6,7},{7,8},{8,9},{9,10},{10,1... | collective-permute-start | bytes 884744 | tf_op jit(solution)/shard_map/while/body/eval_jaxpr/ppermute | solution.py:19
  679.7 18.0 %collective-permute-start.1 = (f32[128,1152]{1,0:T(8,128)S(1)}, f32[128,1152]{1,0:T(8,128)S(1)}, u32[]{:S(2)}, u32[]{:S(2)}) collective-permute-start(f32[128,1152]{1,0:T(8,128)S(1)} %fusion.68), channel_id=1, source_target_pairs={{0,1},{1,2},{2,3},{3,4},{4,5},{5,6},{6,7},{7,8},{8,9},{9,10},{10,1... | collective-permute-start | bytes 1769480 | tf_op jit(solution)/shard_map/while/body/eval_jaxpr/ppermute | solution.py:19
  (42 other events, 736.4 us)
Sparse Core Ops, SparseCore 0:
  11.7 119.6 all-gather.2
where the time goes:
time: 757 us; the launch traced here: 756 us
  waiting for transfers between devices  680 us (90%)
  matrix products  34 us (4%)
  local copies, waits for them, and re-layouts  18.3 us (2%)
  between operations  14.2 us (2%)
    ppermute x63, waiting for transfers between devices, from_behind(): return lax.ppermute(value, axis, pairs)  556 us
    all_gather x1, waiting for transfers between devices, per_device(): whole = lax.all_gather(projections, 'dp', axis=0, tiled=True)  123 us
  transfers between devices with their start and end apart: 64, of which 33 were waited for; matrix products, arithmetic and copies ran while one was open for 1% of the time, Pallas kernels for 0%

commit v1 on v0

v1 whole, which is shorter than its diff:
```python
import jax
import jax.numpy as jnp
from jax import lax
from jax.sharding import Mesh, PartitionSpec as P

AXES = ("x", "z", "y", "c")
SIZES = (4, 8, 4, 2)
WINDOW_PLANES = 4

logit_scale = 10.0
logit_bias = -2.0
eps = 1e-06
contract_last = (((1,), (1,)), ((), ()))
contract_first = (((0,), (0,)), ((), ()))


def along(value, axis, steps):
    count = lax.axis_size(axis)
    return lax.ppermute(value, axis, [(i, (i + steps) % count) for i in range(count)])


def blocks_behind(value, steps):
    return lax.ppermute(value, AXES, [(i, (i + steps) % 256) for i in range(256)])


def normalize(raw):
    norm = jnp.sqrt(jnp.sum(raw * raw, axis=-1, keepdims=True) + eps)
    return (raw / norm, norm)


def unproject(unit, norm, grad):
    inner = jnp.sum(unit * grad, axis=-1, keepdims=True)
    return ((grad - unit * inner) / norm).astype(jnp.bfloat16)


def gather_images(value):
    same = [value, along(value, "y", -1), along(value, "y", 2), along(value, "y", 1)]
    other = [along(v, "c", 1) for v in same]
    return [v for pair in zip(same, other) for v in pair]


def gather_labels(labels):
    pair = jnp.stack([labels, along(labels, "c", 1)])
    around = [pair, along(pair, "y", -1), along(pair, "y", 2), along(pair, "y", 1)]
    return jnp.concatenate(around, axis=0)


def per_device(image_features, text_features, projections, labels):
    rows, width_in = image_features.shape
    x, z, y, c = (lax.axis_index(a) for a in AXES)
    index = lax.axis_index(AXES)
    place = 2 * y + c

    whole = lax.all_gather(projections, AXES, axis=0, tiled=True)
    image_weight = whole[:width_in]
    text_weight = whole[width_in:]

    texts = [text_features]
    for _ in range(WINDOW_PLANES):
        texts.append(blocks_behind(texts[-1], 8))
    images = gather_images(image_features)
    label_slots = gather_labels(labels)

    image_raw = jnp.dot(jnp.concatenate(images, axis=0), image_weight, preferred_element_type=jnp.float32)
    text_raw = jnp.dot(jnp.concatenate(texts, axis=0), text_weight, preferred_element_type=jnp.float32)
    image_unit, image_norm = normalize(image_raw)
    text_unit, text_norm = normalize(text_raw)
    image_emb = image_unit.astype(jnp.bfloat16)
    text_emb = text_unit.astype(jnp.bfloat16)

    slots = jnp.arange(8, dtype=jnp.int32)
    slot_place = 2 * ((y + slots // 2) % 4) + (c + slots) % 2
    planes = jnp.arange(WINDOW_PLANES + 1, dtype=jnp.int32)
    valid = jnp.where(
        planes[None, :] == 0,
        slot_place[:, None] >= place,
        (planes[None, :] < WINDOW_PLANES) | (slot_place[:, None] < place),
    )
    text_ids = ((index - 8 * planes) % 256)[:, None] * rows + jnp.arange(rows, dtype=jnp.int32)
    text_ids = text_ids.reshape(1, 1, WINDOW_PLANES + 1, rows)
    logits = (
        logit_scale
        * lax.dot_general(image_emb, text_emb, contract_last, preferred_element_type=jnp.float32)
        + logit_bias
    ).reshape(8, rows, WINDOW_PLANES + 1, rows)
    positive = (label_slots[:, :, None, None] == text_ids).astype(jnp.float32)
    coeff = jnp.where(valid[:, None, :, None], jax.nn.sigmoid(logits) - positive, 0.0)
    coeff = coeff.astype(jnp.bfloat16).reshape(8 * rows, (WINDOW_PLANES + 1) * rows)

    text_part = lax.dot_general(coeff, image_emb, contract_first, preferred_element_type=jnp.float32)
    image_part = jnp.dot(coeff, text_emb, preferred_element_type=jnp.float32)

    text_part = text_part.reshape(WINDOW_PLANES + 1, rows, -1)
    carried = text_part[WINDOW_PLANES]
    for plane in range(WINDOW_PLANES - 1, -1, -1):
        carried = blocks_behind(carried.astype(jnp.bfloat16), -8).astype(jnp.float32) + text_part[plane]
    text_acc = logit_scale * carried

    image_part = image_part.reshape(4, 2, rows, -1)
    swapped = along(image_part[:, 1].astype(jnp.bfloat16), "c", 1).astype(jnp.float32)
    chip_sum = image_part[:, 0] + swapped
    outgoing = chip_sum.astype(jnp.bfloat16)
    image_acc = chip_sum[0]
    for dy, steps in ((1, 1), (2, 2), (3, -1)):
        image_acc = image_acc + along(outgoing[dy], "y", steps).astype(jnp.float32)
    image_acc = logit_scale * image_acc

    image_draw = unproject(image_unit[:rows], image_norm[:rows], image_acc)
    text_draw = unproject(text_unit[:rows], text_norm[:rows], text_acc)
    image_grad = lax.dot_general(image_draw, image_weight, contract_last, preferred_element_type=jnp.float32)
    text_grad = lax.dot_general(text_draw, text_weight, contract_last, preferred_element_type=jnp.float32)
    return (image_grad, text_grad)


def solution(mesh):
    fine = Mesh(mesh.devices.reshape(SIZES), AXES)
    rows = P(AXES, None)
    return jax.shard_map(
        per_device,
        mesh=fine,
        in_specs=(rows, rows, rows, P(AXES)),
        out_specs=(rows, rows),
        check_vma=False,
    )
```

time: 757 us -> 236 us (0.31)
  waiting for transfers between devices: 680 us -> 127 us
  starting transfers between devices: 6.79 us -> 38.7 us
  matrix products: 34 us -> 20.9 us
  local copies, waits for them, and re-layouts: 18.3 us -> 30.8 us
    ppermute x63 -> x23, waiting for transfers between devices: 556 us -> 65.2 us  [the longest x8 51.7 us: blocks_behind(): lax.ppermute(value, AXES, [(i, (i + steps) % 256) for i in range(256)])]
    all_gather x1, waiting for transfers between devices: 123 us -> 61.4 us  [per_device(): whole = lax.all_gather(projections, AXES, axis=0, tiled=True)]
    ppermute x63 -> x23, starting transfers between devices: 6.75 us -> 38.6 us  [the longest x8 25.5 us: blocks_behind(): lax.ppermute(value, AXES, [(i, (i + steps) % 256) for i in range(256)])]
    dot_general x98 -> x5, matrix products: 30.4 us -> 17.3 us  [the longest x1 6.1 us: per_device(): jnp.dot(jnp.concatenate(images, axis=0), image_weight, preferred_element_...]
  transfers between devices with their start and end apart: 64 -> 24, of which waited for: 33 -> 12; matrix products, arithmetic and copies ran while one was open for 1% -> 7% of each run, Pallas kernels for 0% -> 0%
where the time goes in v1:
time: 236 us; the launch traced here: 234 us
  waiting for transfers between devices  127 us (54%)
  starting transfers between devices  38.7 us (16%)
  local copies, waits for them, and re-layouts  30.8 us (13%)
  matrix products  20.9 us (9%)
  between operations  14.3 us (6%)
  other arithmetic  2.47 us (1%)
    all_gather x1, waiting for transfers between devices, per_device(): whole = lax.all_gather(projections, AXES, axis=0, tiled=True)  61.4 us
    ppermute x8, waiting for transfers between devices, blocks_behind(): lax.ppermute(value, AXES, [(i, (i + steps) % 256) for i in range(256)])  51.7 us
    ppermute x8, starting transfers between devices, blocks_behind(): lax.ppermute(value, AXES, [(i, (i + steps) % 256) for i in range(256)])  25.5 us
    slice x2, local copies, waits for them, and re-layouts, per_device(): text_weight = whole[width_in:]  13.9 us
    ppermute x15, waiting for transfers between devices, along(): lax.ppermute(value, axis, [(i, (i + steps) % count) for i in range(count)])  13.5 us
    ppermute x15, starting transfers between devices, along(): lax.ppermute(value, axis, [(i, (i + steps) % count) for i in range(count)])  13.1 us
    unnamed x26, local copies, waits for them, and re-layouts  8.19 us
    dot_general x1, matrix products, per_device(): jnp.dot(jnp.concatenate(images, axis=0), image_weight, preferred_element_...  6.1 us
  transfers between devices with their start and end apart: 24, of which 12 were waited for; matrix products, arithmetic and copies ran while one was open for 7% of the time, Pallas kernels for 0%

profile of v1, /device:TPU:0, one launch (start us, length us, event | category | flops | bytes accessed | tf_op | source)
XLA Modules:
  0.0 234.4 jit_solution(5961108875272156697)
XLA Ops:
  7.9 1.5 collective-permute-start.3
  10.5 1.9 collective-permute-start.7
  13.5 1.7 constant_dynamic-update-slice_fusion.7
  17.7 3.0 %collective-permute-done.14 = s32[2,128]{1,0:T(2,128)S(1)} collective-permute-done((s32[2,128]{1,0:T(2,128)S(1)}, s32[2,128]{1,0:T(2,128)S(1)}, u32[]{:S(2)}, u32[]{:S(2)}) %collective-permute-start.14) | collective-permute-done | bytes 1056 | tf_op jit(solution)/shard_map/ppermute | solution.py:19
  21.9 4.2 %collective-permute-start.12 = (s32[2,128]{1,0:T(2,128)S(1)}, s32[2,128]{1,0:T(2,128)S(1)}, u32[]{:S(2)}, u32[]{:S(2)}) collective-permute-start(s32[2,128]{1,0:T(2,128)S(1)} %pad_add_fusion), channel_id=1, source_target_pairs={{0,6},{2,0},{4,2},{6,4},{1,7},{3,1},{5,3},{7,5},{8,14},{10,8},{12,... | collective-permute-start | bytes 3080 | tf_op jit(solution)/shard_map/ppermute | solution.py:19
  26.1 1.3 collective-permute-done.12
  28.1 1.6 copy.11
  29.7 2.0 collective-permute-start.8
  34.0 11.9 %collective-permute-done.8 = bf16[128,1152]{1,0:T(8,128)(2,1)S(1)} collective-permute-done((bf16[128,1152]{1,0:T(8,128)(2,1)S(1)}, bf16[128,1152]{1,0:T(8,128)(2,1)S(1)}, u32[]{:S(2)}, u32[]{:S(2)}) %collective-permute-start.8) | collective-permute-done | bytes 294944 | tf_op jit(solution)/shard_map/ppermute | solution.py:23
  48.8 9.3 %collective-permute-done.9 = bf16[128,1152]{1,0:T(8,128)(2,1)S(1)} collective-permute-done((bf16[128,1152]{1,0:T(8,128)(2,1)S(1)}, bf16[128,1152]{1,0:T(8,128)(2,1)S(1)}, u32[]{:S(2)}, u32[]{:S(2)}) %collective-permute-start.9) | collective-permute-done | bytes 294944 | tf_op jit(solution)/shard_map/ppermute | solution.py:23
  58.9 11.2 %collective-permute-done.10 = bf16[128,1152]{1,0:T(8,128)(2,1)S(1)} collective-permute-done((bf16[128,1152]{1,0:T(8,128)(2,1)S(1)}, bf16[128,1152]{1,0:T(8,128)(2,1)S(1)}, u32[]{:S(2)}, u32[]{:S(2)}) %collective-permute-start.10) | collective-permute-done | bytes 294944 | tf_op jit(solution)/shard_map/ppermute | solution.py:23
  70.1 61.4 %all-gather.3.cloned.1.call-done = bf16[256,9,1152]{2,1,0:T(8,128)(2,1)} async-done(((bf16[1,9,1152]{2,1,0:T(8,128)(2,1)}), bf16[256,9,1152]{2,1,0:T(8,128)(2,1)}) %all-gather.3.cloned.1.call-update) | async-done | bytes 5308432 | tf_op jit(solution)/shard_map/all_gather | solution.py:54
  131.5 8.2 %fusion.39 = (bf16[128,9,1152]{2,1,0:T(8,128)(2,1)}, bf16[128,9,1152]{2,1,0:T(8,128)(2,1)}) fusion(bf16[256,9,1152]{2,1,0:T(8,128)(2,1)} %all-gather.3.cloned.1.call-done), kind=kLoop, calls=%fused_computation.92 | loop fusion | bytes 10616832 | tf_op jit(solution)/shard_map/slice | solution.py:56
  139.7 5.7 %reshape.210 = bf16[1152,1152]{1,0:T(8,128)(2,1)} reshape(bf16[128,9,1152]{2,1,0:T(8,128)(2,1)} %get-tuple-element.4) | data formatting | bytes 5308416 | tf_op jit(solution)/shard_map/slice | solution.py:56
  145.4 4.5 %multiply_reduce_fusion.1 = (f32[640]{0:T(1024)S(1)}, f32[640,1152]{1,0:T(8,128)S(1)}) fusion(bf16[640,1152]{1,0:T(8,128)(2,1)} %copy-done.3, bf16[1152,1152]{1,0:T(8,128)(2,1)} %reshape.210), kind=kOutput, calls=%fused_computation.1 | convolution fusion | flops 1700167040 | bytes 7080448 | tf_op jit(solution)/shard_map/dot_general | solution.py:65
  150.0 5.7 %reshape.209 = bf16[1152,1152]{1,0:T(8,128)(2,1)} reshape(bf16[128,9,1152]{2,1,0:T(8,128)(2,1)} %get-tuple-element.5) | data formatting | bytes 5308416 | tf_op jit(solution)/shard_map/slice | solution.py:55
  155.7 6.1 %multiply_reduce_fusion = (f32[1024]{0:T(1024)S(1)}, f32[1024,1152]{1,0:T(8,128)S(1)}) fusion(bf16[1024,1152]{1,0:T(8,128)(2,1)} %constant_dynamic-update-slice_fusion, bf16[1152,1152]{1,0:T(8,128)(2,1)} %reshape.209), kind=kOutput, calls=%fused_computation | convolution fusion | flops 2720267264 | bytes 9736192 | tf_op jit(solution)/shard_map/dot_general | solution.py:64
  163.2 2.6 %select_convert_fusion = bf16[1024,640]{1,0:T(8,128)(2,1)S(1)} fusion(pred[1024,640]{1,0:T(32,128)(4,1)S(1)} %copy-done.2, s32[640]{0:T(1024)S(1)} %bitcast_add_fusion, s32[1024]{0:T(1024)S(1)} %bitcast.58, f32[1024,1152]{1,0:T(8,128)S(1)} %broadcast_divide_fusion, f32[640,1152]{1,0:T(8,128)S(1)} %broadcast_divide_fusion.1), kind=kOutput, calls=%fused_computation.2 | convolution fusion | flops 1518419968 | bytes 9640448 | tf_op jit(solution)/shard_map/dot_general | solution.py:83
  165.8 1.9 fusion.5
  167.8 3.7 %collective-permute-start.19 = (bf16[128,1152]{1,0:T(8,128)(2,1)S(1)}, bf16[128,1152]{1,0:T(8,128)(2,1)S(1)}, u32[]{:S(2)}, u32[]{:S(2)}) collective-permute-start(bf16[128,1152]{1,0:T(8,128)(2,1)S(1)} %slice.141), channel_id=1, source_target_pairs={{0,248},{1,249},{2,250},{3,251},{4,252},{5,253},{6,254},{7,255},{8... | collective-permute-start | bytes 884744 | tf_op jit(solution)/shard_map/ppermute | solution.py:23
  171.6 6.7 %collective-permute-done.19 = bf16[128,1152]{1,0:T(8,128)(2,1)S(1)} collective-permute-done((bf16[128,1152]{1,0:T(8,128)(2,1)S(1)}, bf16[128,1152]{1,0:T(8,128)(2,1)S(1)}, u32[]{:S(2)}, u32[]{:S(2)}) %collective-permute-start.19) | collective-permute-done | bytes 294944 | tf_op jit(solution)/shard_map/ppermute | solution.py:23
  178.3 6.1 %collective-permute-start.20 = (bf16[128,1152]{1,0:T(8,128)(2,1)S(1)}, bf16[128,1152]{1,0:T(8,128)(2,1)S(1)}, u32[]{:S(2)}, u32[]{:S(2)}) collective-permute-start(bf16[128,1152]{1,0:T(8,128)(2,1)S(1)} %fusion.16), channel_id=1, source_target_pairs={{0,248},{1,249},{2,250},{3,251},{4,252},{5,253},{6,254},{7,255},{8... | collective-permute-start | bytes 884744 | tf_op jit(solution)/shard_map/ppermute | solution.py:23
  184.4 2.2 fusion.1
  186.6 3.7 %collective-permute-done.20 = bf16[128,1152]{1,0:T(8,128)(2,1)S(1)} collective-permute-done((bf16[128,1152]{1,0:T(8,128)(2,1)S(1)}, bf16[128,1152]{1,0:T(8,128)(2,1)S(1)}, u32[]{:S(2)}, u32[]{:S(2)}) %collective-permute-start.20) | collective-permute-done | bytes 294944 | tf_op jit(solution)/shard_map/ppermute | solution.py:23
  190.4 5.9 %collective-permute-start.21 = (bf16[128,1152]{1,0:T(8,128)(2,1)S(1)}, bf16[128,1152]{1,0:T(8,128)(2,1)S(1)}, u32[]{:S(2)}, u32[]{:S(2)}) collective-permute-start(bf16[128,1152]{1,0:T(8,128)(2,1)S(1)} %fusion.15), channel_id=1, source_target_pairs={{0,248},{1,249},{2,250},{3,251},{4,252},{5,253},{6,254},{7,255},{8... | collective-permute-start | bytes 884744 | tf_op jit(solution)/shard_map/ppermute | solution.py:23
  196.5 4.7 %collective-permute-done.21 = bf16[128,1152]{1,0:T(8,128)(2,1)S(1)} collective-permute-done((bf16[128,1152]{1,0:T(8,128)(2,1)S(1)}, bf16[128,1152]{1,0:T(8,128)(2,1)S(1)}, u32[]{:S(2)}, u32[]{:S(2)}) %collective-permute-start.21) | collective-permute-done | bytes 294944 | tf_op jit(solution)/shard_map/ppermute | solution.py:23
  201.3 5.9 %collective-permute-start.22 = (bf16[128,1152]{1,0:T(8,128)(2,1)S(1)}, bf16[128,1152]{1,0:T(8,128)(2,1)S(1)}, u32[]{:S(2)}, u32[]{:S(2)}) collective-permute-start(bf16[128,1152]{1,0:T(8,128)(2,1)S(1)} %fusion.14), channel_id=1, source_target_pairs={{0,248},{1,249},{2,250},{3,251},{4,252},{5,253},{6,254},{7,255},{8... | collective-permute-start | bytes 884744 | tf_op jit(solution)/shard_map/ppermute | solution.py:23
  207.1 4.2 %collective-permute-done.22 = bf16[128,1152]{1,0:T(8,128)(2,1)S(1)} collective-permute-done((bf16[128,1152]{1,0:T(8,128)(2,1)S(1)}, bf16[128,1152]{1,0:T(8,128)(2,1)S(1)}, u32[]{:S(2)}, u32[]{:S(2)}) %collective-permute-start.22) | collective-permute-done | bytes 294944 | tf_op jit(solution)/shard_map/ppermute | solution.py:23
  212.3 3.0 %collective-permute-start.18 = (bf16[128,1152]{1,0:T(8,128)(2,1)S(1)}, bf16[128,1152]{1,0:T(8,128)(2,1)S(1)}, u32[]{:S(2)}, u32[]{:S(2)}) collective-permute-start(bf16[128,1152]{1,0:T(8,128)(2,1)S(1)} %get-tuple-element.7), channel_id=1, source_target_pairs={{0,6},{2,0},{4,2},{6,4},{1,7},{3,1},{5,3},{7,5},{8,14},{10,8},{12,... | collective-permute-start | bytes 884744 | tf_op jit(solution)/shard_map/ppermute | solution.py:19
  215.7 1.8 fusion.22
  217.5 7.9 %collective-permute-done.16 = bf16[128,1152]{1,0:T(8,128)(2,1)S(1)} collective-permute-done((bf16[128,1152]{1,0:T(8,128)(2,1)S(1)}, bf16[128,1152]{1,0:T(8,128)(2,1)S(1)}, u32[]{:S(2)}, u32[]{:S(2)}) %collective-permute-start.16) | collective-permute-done | bytes 294944 | tf_op jit(solution)/shard_map/ppermute | solution.py:19
  225.7 1.8 fusion.21
  (82 shorter events, 16.7 us)
Async XLA Ops:
  7.2 22.5 %copy-start.6 = (s32[128]{0:T(128)S(1)}, s32[128]{0:T(128)}, u32[]{:S(2)}) copy-start(s32[128]{0:T(128)} %param.7) | copy-start | bytes 1540
  7.2 124.3 %all-gather.3.cloned.1.call-start = ((), (), s32[]{:S(2)}) async-start(), calls=%async_computation | async-start | bytes 9474048 | tf_op jit(solution)/shard_map/all_gather | solution.py:54
  7.9 23.8 %collective-permute-start.3 = (bf16[128,1152]{1,0:T(8,128)(2,1)}, bf16[128,1152]{1,0:T(8,128)(2,1)S(1)}, u32[]{:S(2)}, u32[]{:S(2)}) collective-permute-start(bf16[128,1152]{1,0:T(8,128)(2,1)} %param.4), channel_id=1, source_target_pairs={{0,4},{2,6},{4,0},{6,2},{1,5},{3,7},{5,1},{7,3},{8,12},{10,14},{12... | collective-permute-start | bytes 884744 | tf_op jit(solution)/shard_map/ppermute | solution.py:19
  9.5 22.5 %collective-permute-start.1 = (bf16[128,1152]{1,0:T(8,128)(2,1)}, bf16[128,1152]{1,0:T(8,128)(2,1)S(1)}, u32[]{:S(2)}, u32[]{:S(2)}) collective-permute-start(bf16[128,1152]{1,0:T(8,128)(2,1)} %param.4), channel_id=1, source_target_pairs={{0,6},{2,0},{4,2},{6,4},{1,7},{3,1},{5,3},{7,5},{8,14},{10,8},{12,... | collective-permute-start | bytes 884744 | tf_op jit(solution)/shard_map/ppermute | solution.py:19
  10.5 4.7 %collective-permute-start.11 = (s32[128]{0:T(128)}, s32[128]{0:T(128)S(1)}, u32[]{:S(2)}, u32[]{:S(2)}) collective-permute-start(s32[128]{0:T(128)} %param.7), channel_id=1, source_target_pairs={{0,1},{1,0},{2,3},{3,2},{4,5},{5,4},{6,7},{7,6},{8,9},{9,8},{10,11... | collective-permute-start | bytes 1544 | tf_op jit(solution)/shard_map/ppermute | solution.py:19
  10.5 19.2 %collective-permute-start.7 = (bf16[128,1152]{1,0:T(8,128)(2,1)}, bf16[128,1152]{1,0:T(8,128)(2,1)S(1)}, u32[]{:S(2)}, u32[]{:S(2)}) collective-permute-start(bf16[128,1152]{1,0:T(8,128)(2,1)} %param.5), channel_id=1, source_target_pairs={{0,8},{1,9},{2,10},{3,11},{4,12},{5,13},{6,14},{7,15},{8,16},{9,17... | collective-permute-start | bytes 884744 | tf_op jit(solution)/shard_map/ppermute | solution.py:23
  15.9 4.8 %collective-permute-start.14 = (s32[2,128]{1,0:T(2,128)S(1)}, s32[2,128]{1,0:T(2,128)S(1)}, u32[]{:S(2)}, u32[]{:S(2)}) collective-permute-start(s32[2,128]{1,0:T(2,128)S(1)} %pad_add_fusion), channel_id=1, source_target_pairs={{0,2},{2,4},{4,6},{6,0},{1,3},{3,5},{5,7},{7,1},{8,10},{10,12},{12... | collective-permute-start | bytes 3080 | tf_op jit(solution)/shard_map/ppermute | solution.py:19
  16.9 5.1 %collective-permute-start.13 = (s32[2,128]{1,0:T(2,128)S(1)}, s32[2,128]{1,0:T(2,128)S(1)}, u32[]{:S(2)}, u32[]{:S(2)}) collective-permute-start(s32[2,128]{1,0:T(2,128)S(1)} %pad_add_fusion), channel_id=1, source_target_pairs={{0,4},{2,6},{4,0},{6,2},{1,5},{3,7},{5,1},{7,3},{8,12},{10,14},{12... | collective-permute-start | bytes 3080 | tf_op jit(solution)/shard_map/ppermute | solution.py:19
  20.7 11.5 %collective-permute-start.5 = (bf16[128,1152]{1,0:T(8,128)(2,1)}, bf16[128,1152]{1,0:T(8,128)(2,1)S(1)}, u32[]{:S(2)}, u32[]{:S(2)}) collective-permute-start(bf16[128,1152]{1,0:T(8,128)(2,1)} %param.4), channel_id=1, source_target_pairs={{0,2},{2,4},{4,6},{6,0},{1,3},{3,5},{5,7},{7,1},{8,10},{10,12},{12... | collective-permute-start | bytes 884744 | tf_op jit(solution)/shard_map/ppermute | solution.py:19
  21.9 5.5 %collective-permute-start.12 = (s32[2,128]{1,0:T(2,128)S(1)}, s32[2,128]{1,0:T(2,128)S(1)}, u32[]{:S(2)}, u32[]{:S(2)}) collective-permute-start(s32[2,128]{1,0:T(2,128)S(1)} %pad_add_fusion), channel_id=1, source_target_pairs={{0,6},{2,0},{4,2},{6,4},{1,7},{3,1},{5,3},{7,5},{8,14},{10,8},{12,... | collective-permute-start | bytes 3080 | tf_op jit(solution)/shard_map/ppermute | solution.py:19
  27.4 5.1 %collective-permute-start = (bf16[128,1152]{1,0:T(8,128)(2,1)}, bf16[128,1152]{1,0:T(8,128)(2,1)S(1)}, u32[]{:S(2)}, u32[]{:S(2)}) collective-permute-start(bf16[128,1152]{1,0:T(8,128)(2,1)} %param.4), channel_id=1, source_target_pairs={{0,1},{1,0},{2,3},{3,2},{4,5},{5,4},{6,7},{7,6},{8,9},{9,8},{10,11... | collective-permute-start | bytes 884744 | tf_op jit(solution)/shard_map/ppermute | solution.py:19
  29.7 16.1 %collective-permute-start.8 = (bf16[128,1152]{1,0:T(8,128)(2,1)S(1)}, bf16[128,1152]{1,0:T(8,128)(2,1)S(1)}, u32[]{:S(2)}, u32[]{:S(2)}) collective-permute-start(bf16[128,1152]{1,0:T(8,128)(2,1)S(1)} %collective-permute-done.7), channel_id=1, source_target_pairs={{0,8},{1,9},{2,10},{3,11},{4,12},{5,13},{6,14},{7,15},{8,16},{9,17... | collective-permute-start | bytes 884744 | tf_op jit(solution)/shard_map/ppermute | solution.py:23
  31.7 15.7 %collective-permute-start.4 = (bf16[128,1152]{1,0:T(8,128)(2,1)S(1)}, bf16[128,1152]{1,0:T(8,128)(2,1)S(1)}, u32[]{:S(2)}, u32[]{:S(2)}) collective-permute-start(bf16[128,1152]{1,0:T(8,128)(2,1)S(1)} %collective-permute-done.3), channel_id=1, source_target_pairs={{0,1},{1,0},{2,3},{3,2},{4,5},{5,4},{6,7},{7,6},{8,9},{9,8},{10,11... | collective-permute-start | bytes 884744 | tf_op jit(solution)/shard_map/ppermute | solution.py:19
  31.9 13.9 %collective-permute-start.2 = (bf16[128,1152]{1,0:T(8,128)(2,1)S(1)}, bf16[128,1152]{1,0:T(8,128)(2,1)S(1)}, u32[]{:S(2)}, u32[]{:S(2)}) collective-permute-start(bf16[128,1152]{1,0:T(8,128)(2,1)S(1)} %collective-permute-done.1), channel_id=1, source_target_pairs={{0,1},{1,0},{2,3},{3,2},{4,5},{5,4},{6,7},{7,6},{8,9},{9,8},{10,11... | collective-permute-start | bytes 884744 | tf_op jit(solution)/shard_map/ppermute | solution.py:19
  32.2 25.9 %collective-permute-start.6 = (bf16[128,1152]{1,0:T(8,128)(2,1)S(1)}, bf16[128,1152]{1,0:T(8,128)(2,1)S(1)}, u32[]{:S(2)}, u32[]{:S(2)}) collective-permute-start(bf16[128,1152]{1,0:T(8,128)(2,1)S(1)} %collective-permute-done.5), channel_id=1, source_target_pairs={{0,1},{1,0},{2,3},{3,2},{4,5},{5,4},{6,7},{7,6},{8,9},{9,8},{10,11... | collective-permute-start | bytes 884744 | tf_op jit(solution)/shard_map/ppermute | solution.py:19
  45.9 12.3 %collective-permute-start.9 = (bf16[128,1152]{1,0:T(8,128)(2,1)S(1)}, bf16[128,1152]{1,0:T(8,128)(2,1)S(1)}, u32[]{:S(2)}, u32[]{:S(2)}) collective-permute-start(bf16[128,1152]{1,0:T(8,128)(2,1)S(1)} %collective-permute-done.8), channel_id=1, source_target_pairs={{0,8},{1,9},{2,10},{3,11},{4,12},{5,13},{6,14},{7,15},{8,16},{9,17... | collective-permute-start | bytes 884744 | tf_op jit(solution)/shard_map/ppermute | solution.py:23
  58.1 12.0 %collective-permute-start.10 = (bf16[128,1152]{1,0:T(8,128)(2,1)S(1)}, bf16[128,1152]{1,0:T(8,128)(2,1)S(1)}, u32[]{:S(2)}, u32[]{:S(2)}) collective-permute-start(bf16[128,1152]{1,0:T(8,128)(2,1)S(1)} %collective-permute-done.9), channel_id=1, source_target_pairs={{0,8},{1,9},{2,10},{3,11},{4,12},{5,13},{6,14},{7,15},{8,16},{9,17... | collective-permute-start | bytes 884744 | tf_op jit(solution)/shard_map/ppermute | solution.py:23
  70.1 69.5 %copy-start.3 = (bf16[640,1152]{1,0:T(8,128)(2,1)}, bf16[640,1152]{1,0:T(8,128)(2,1)S(1)}, u32[]{:S(2)}) copy-start(bf16[640,1152]{1,0:T(8,128)(2,1)S(1)} %constant_dynamic-update-slice_fusion.8) | copy-start | bytes 4423684
  150.0 57.2 %copy-start.4 = (f32[640]{0:T(1024)}, f32[640]{0:T(1024)S(1)}, u32[]{:S(2)}) copy-start(f32[640]{0:T(1024)S(1)} %add_sqrt_fusion) | copy-start | bytes 7684
  161.8 45.3 %copy-start.5 = (f32[1024]{0:T(1024)}, f32[1024]{0:T(1024)S(1)}, u32[]{:S(2)}) copy-start(f32[1024]{0:T(1024)S(1)} %add_sqrt_fusion.1) | copy-start | bytes 12292
  167.8 10.4 %collective-permute-start.19 = (bf16[128,1152]{1,0:T(8,128)(2,1)S(1)}, bf16[128,1152]{1,0:T(8,128)(2,1)S(1)}, u32[]{:S(2)}, u32[]{:S(2)}) collective-permute-start(bf16[128,1152]{1,0:T(8,128)(2,1)S(1)} %slice.141), channel_id=1, source_target_pairs={{0,248},{1,249},{2,250},{3,251},{4,252},{5,253},{6,254},{7,255},{8... | collective-permute-start | bytes 884744 | tf_op jit(solution)/shard_map/ppermute | solution.py:23
  178.3 12.0 %collective-permute-start.20 = (bf16[128,1152]{1,0:T(8,128)(2,1)S(1)}, bf16[128,1152]{1,0:T(8,128)(2,1)S(1)}, u32[]{:S(2)}, u32[]{:S(2)}) collective-permute-start(bf16[128,1152]{1,0:T(8,128)(2,1)S(1)} %fusion.16), channel_id=1, source_target_pairs={{0,248},{1,249},{2,250},{3,251},{4,252},{5,253},{6,254},{7,255},{8... | collective-permute-start | bytes 884744 | tf_op jit(solution)/shard_map/ppermute | solution.py:23
  190.4 10.8 %collective-permute-start.21 = (bf16[128,1152]{1,0:T(8,128)(2,1)S(1)}, bf16[128,1152]{1,0:T(8,128)(2,1)S(1)}, u32[]{:S(2)}, u32[]{:S(2)}) collective-permute-start(bf16[128,1152]{1,0:T(8,128)(2,1)S(1)} %fusion.15), channel_id=1, source_target_pairs={{0,248},{1,249},{2,250},{3,251},{4,252},{5,253},{6,254},{7,255},{8... | collective-permute-start | bytes 884744 | tf_op jit(solution)/shard_map/ppermute | solution.py:23
  196.4 15.2 %collective-permute-start.15 = (bf16[4,128,1152]{2,1,0:T(8,128)(2,1)S(1)}, bf16[4,128,1152]{2,1,0:T(8,128)(2,1)S(1)}, u32[]{:S(2)}, u32[]{:S(2)}) collective-permute-start(bf16[4,128,1152]{2,1,0:T(8,128)(2,1)S(1)} %fusion.4), channel_id=1, source_target_pairs={{0,1},{1,0},{2,3},{3,2},{4,5},{5,4},{6,7},{7,6},{8,9},{9,8},{10,11... | collective-permute-start | bytes 3538952 | tf_op jit(solution)/shard_map/ppermute | solution.py:19
  201.3 10.1 %collective-permute-start.22 = (bf16[128,1152]{1,0:T(8,128)(2,1)S(1)}, bf16[128,1152]{1,0:T(8,128)(2,1)S(1)}, u32[]{:S(2)}, u32[]{:S(2)}) collective-permute-start(bf16[128,1152]{1,0:T(8,128)(2,1)S(1)} %fusion.14), channel_id=1, source_target_pairs={{0,248},{1,249},{2,250},{3,251},{4,252},{5,253},{6,254},{7,255},{8... | collective-permute-start | bytes 884744 | tf_op jit(solution)/shard_map/ppermute | solution.py:23
  211.6 4.2 %copy-start.1 = (bf16[1152,1152]{1,0:T(8,128)(2,1)S(1)}, bf16[1152,1152]{1,0:T(8,128)(2,1)}, u32[]{:S(2)}) copy-start(bf16[1152,1152]{1,0:T(8,128)(2,1)} %reshape.210) | copy-start | bytes 7962628
  211.6 4.2 %slice-start = ((f32[640]{0:T(1024)}), f32[128]{0:T(128)S(1)}, s32[]{:S(2)}) async-start(f32[640]{0:T(1024)} %copy-done.4), calls=%async_computation.1 | async-start | bytes 1024 | tf_op jit(solution)/shard_map/slice | solution.py:109
  212.0 13.4 %collective-permute-start.16 = (bf16[128,1152]{1,0:T(8,128)(2,1)S(1)}, bf16[128,1152]{1,0:T(8,128)(2,1)S(1)}, u32[]{:S(2)}, u32[]{:S(2)}) collective-permute-start(bf16[128,1152]{1,0:T(8,128)(2,1)S(1)} %get-tuple-element.6), channel_id=1, source_target_pairs={{0,2},{2,4},{4,6},{6,0},{1,3},{3,5},{5,7},{7,1},{8,10},{10,12},{12... | collective-permute-start | bytes 884744 | tf_op jit(solution)/shard_map/ppermute | solution.py:19
  212.3 13.1 %collective-permute-start.18 = (bf16[128,1152]{1,0:T(8,128)(2,1)S(1)}, bf16[128,1152]{1,0:T(8,128)(2,1)S(1)}, u32[]{:S(2)}, u32[]{:S(2)}) collective-permute-start(bf16[128,1152]{1,0:T(8,128)(2,1)S(1)} %get-tuple-element.7), channel_id=1, source_target_pairs={{0,6},{2,0},{4,2},{6,4},{1,7},{3,1},{5,3},{7,5},{8,14},{10,8},{12,... | collective-permute-start | bytes 884744 | tf_op jit(solution)/shard_map/ppermute | solution.py:19
  215.3 10.4 %copy-start = (bf16[1152,1152]{1,0:T(8,128)(2,1)S(1)}, bf16[1152,1152]{1,0:T(8,128)(2,1)}, u32[]{:S(2)}) copy-start(bf16[1152,1152]{1,0:T(8,128)(2,1)} %reshape.209) | copy-start | bytes 7962628
  215.3 10.4 %slice-start.1 = ((f32[1024]{0:T(1024)}), f32[128]{0:T(128)S(1)}, s32[]{:S(2)}) async-start(f32[1024]{0:T(1024)} %copy-done.5), calls=%async_computation.2 | async-start | bytes 1024 | tf_op jit(solution)/shard_map/slice | solution.py:108
  215.3 10.1 %collective-permute-start.17 = (bf16[128,1152]{1,0:T(8,128)(2,1)S(1)}, bf16[128,1152]{1,0:T(8,128)(2,1)S(1)}, u32[]{:S(2)}, u32[]{:S(2)}) collective-permute-start(bf16[128,1152]{1,0:T(8,128)(2,1)S(1)} %get-tuple-element.8), channel_id=1, source_target_pairs={{0,4},{2,6},{4,0},{6,2},{1,5},{3,7},{5,1},{7,3},{8,12},{10,14},{12... | collective-permute-start | bytes 884744 | tf_op jit(solution)/shard_map/ppermute | solution.py:19
  (1 other events, 1.1 us)
Sparse Core Ops, SparseCore 0:
  11.7 119.7 all-gather.2
